TPU v7x, 32 devices: a whole 2x2x4 slice. The times are simulated.
32 devices in a mesh: parts: 2 (over y), track: 4 (over z), tm: 2 (over x), coef: 2 (over core).
Axes of the slice: x: 2, y: 2, z: 4, core: 2. Of those that a mesh axis runs over, the one named last changes fastest.
Arguments:
- sector_ids: int32 [12288], P(('parts', 'track', 'tm')), parts along dimension 0, may hold values from 0 to 63, as said below
- observed: float32 [3, 12288], P(None, ('parts', 'track', 'tm')), parts along dimension 1, may hold values from -6 to 6
- weights: float32 [3, 12288], P(None, ('parts', 'track', 'tm')), parts along dimension 1, may hold values from 0.3 to 3
- coefficients: float32 [2048, 128], P(('parts', 'track')), parts along dimension 0, may hold values from -6 to 6
- tile_index: int32 [128, 12], P(('parts', 'track', 'tm'), 'coef'), parts along dimension 0, may hold values from 0 to 1023, as said below
- tile_count: int32 [128], P(('parts', 'track', 'tm')), parts along dimension 0, may hold values from 3 to 12
- sensitivity: bfloat16 [128, 12, 3, 128, 128], P(('parts', 'track', 'tm'), 'coef'), parts along dimension 0, may hold values from -0.15625 to 0.15625
Outputs:
- gradient: float32 [2048, 128], P(('parts', 'track')), parts along dimension 0
There are 2 independent parts, one for each index of `parts`. A program takes and returns all parts, laid end to end along the dimension named above; each array names one. Nothing has to cross between parts.
Inputs may be any that keep to these rules, and one draw needn't show every extreme that they name: `sector_ids`: the rows of one index of track and tm fall in at most 192 rows into the 8 consecutive sectors of any one index, and some pair reaches 192; the sectors of each index receive exactly 768 rows in all; each sector holds at most 128 rows, and every index holds a sector with exactly 128. `tile_index`: entries at positions from tile_count on are arbitrary blocks and take no part. Block n belongs to track index n // 256. Of the 48 entries held by one index of track, tm and coef (its sectors' rows, its coef share of the columns), live or not, at most 24 name blocks of any one track index, and every such device has a track index named exactly 24 times.
All inputs are finite; a program needn't handle non-finite values.
Results may differ from a plain program's by a relative error of at most 0.0037.
Values may be sent and summed in bfloat16 or wider, within the bound.
A program may use at most 64 MiB of HBM per device.

v0:
```python
import jax
import jax.numpy as jnp
from jax import lax
from jax.sharding import PartitionSpec as P

HUBER = 2.0


def per_device(sector_ids, observed, weights, coefficients, tile_index, tile_count, sensitivity):
    sector_total = tile_index.shape[0]
    half_k = tile_index.shape[1]
    slot_count = sensitivity.shape[3]
    block_width = sensitivity.shape[4]
    owners = lax.axis_size(("track", "tm"))
    row_total = sector_ids.shape[0]
    capacity = 2 * row_total // owners
    rounded = coefficients.astype(jnp.bfloat16)
    every_block = lax.all_gather(rounded, "track", axis=0, tiled=True)
    owner_of = sector_ids // sector_total
    local_sector = sector_ids % sector_total
    onehot = (owner_of[:, None] == jnp.arange(owners, dtype=jnp.int32)[None, :]).astype(jnp.int32)
    ranking = jnp.sum((jnp.cumsum(onehot, axis=0) - 1) * onehot, axis=1)
    placing = owner_of * capacity + ranking
    payload = jnp.concatenate([observed, weights], axis=0)
    outgoing = jnp.zeros((6, owners * capacity), jnp.float32).at[:, placing].set(payload)
    outgoing = jnp.transpose(outgoing.reshape(6, owners, capacity), (1, 0, 2))
    labels = jnp.full((owners * capacity,), -1, jnp.int32).at[placing].set(local_sector)
    labels = labels.reshape(owners, capacity)
    got_rows, got_labels = (
        lax.all_to_all(outgoing, ("track", "tm"), split_axis=0, concat_axis=0, tiled=True),
        lax.all_to_all(labels, ("track", "tm"), split_axis=0, concat_axis=0, tiled=True),
    )
    received = jnp.transpose(got_rows, (1, 0, 2)).reshape(6, owners * capacity)
    flat_labels = got_labels.reshape(owners * capacity)
    member = (flat_labels[:, None] == jnp.arange(sector_total, dtype=jnp.int32)[None, :]).astype(
        jnp.int32
    )
    within = jnp.sum((jnp.cumsum(member, axis=0) - 1) * member, axis=1)
    target = jnp.where(
        flat_labels >= 0, flat_labels * slot_count + within, sector_total * slot_count
    )
    gridded = jnp.zeros((6, sector_total * slot_count + 1), jnp.float32).at[:, target].set(received)
    gridded = jnp.transpose(gridded[:, :-1].reshape(6, sector_total, slot_count), (1, 0, 2))
    observed_tiles = gridded[:, :3]
    weight_tiles = gridded[:, 3:]
    k_global = lax.axis_index("coef") * half_k + jnp.arange(half_k, dtype=jnp.int32)
    active = k_global[None, :] < tile_count[:, None]
    blocks = jnp.take(every_block, tile_index, axis=0)
    blocks = jnp.where(active[:, :, None], blocks, jnp.zeros_like(blocks))
    partial_pred = jnp.einsum(
        "skcjb,skb->scj", sensitivity, blocks, preferred_element_type=jnp.float32
    )
    predicted = lax.psum(partial_pred, "coef")
    scaled = weight_tiles * (predicted - observed_tiles)
    force = (weight_tiles * scaled / jnp.sqrt(1.0 + (scaled / HUBER) ** 2)).astype(jnp.bfloat16)
    tile_grad = jnp.einsum("skcjb,scj->skb", sensitivity, force, preferred_element_type=jnp.float32)
    tile_grad = jnp.where(active[:, :, None], tile_grad, jnp.zeros_like(tile_grad))
    block_total = every_block.shape[0]
    partial_grad = jnp.zeros((block_total, block_width), jnp.float32)
    partial_grad = partial_grad.at[tile_index.reshape(-1)].add(tile_grad.reshape(-1, block_width))
    summed = lax.psum_scatter(partial_grad, "track", scatter_dimension=0, tiled=True)
    gradient = lax.psum(summed, ("tm", "coef"))
    return gradient


def solution(mesh):
    placed = (
        P(("parts", "track", "tm")),
        P(None, ("parts", "track", "tm")),
        P(None, ("parts", "track", "tm")),
        P(("parts", "track"), None),
        P(("parts", "track", "tm"), "coef"),
        P(("parts", "track", "tm")),
        P(("parts", "track", "tm"), "coef", None, None, None),
    )
    return jax.shard_map(
        per_device,
        mesh=mesh,
        in_specs=placed,
        out_specs=P(("parts", "track"), None),
        check_vma=False,
    )
```

profile of v0, /device:TPU:0, one launch (start us, length us, event | category | flops | bytes accessed | tf_op | source)
XLA Modules:
  0.0 135.0 jit_solution(9949122944024813271)
XLA Ops:
  6.5 0.7 add_select_fusion
  7.2 1.7 %reduce-window.14 = s32[8,6,128]{2,0,1:T(8,128)S(1)} reduce-window(s32[8,6,128]{2,0,1:T(8,128)S(1)} %fusion.13, s32[]{:T(128)} %constant.40.clone.1), window={size=1x1x128 pad=0_0x0_0x127_0}, to_apply=%region_0.1 | reduce-window | flops 780288 | bytes 49156 | tf_op jit(solution)/shard_map/reduce-window
  8.9 0.1 slice.30
  9.0 0.1 copy.24
  9.2 0.2 reduce-window.15
  9.3 0.1 copy.25
  9.4 0.1 fusion.11
  9.5 3.4 %scatter_custom_fusion = s32[1536]{0:T(1024)S(1)} fusion(s32[768]{0:T(1024)S(1)} %compare_select_fusion.2, s32[768]{0:T(1024)S(1)} %get-tuple-element.7, s32[]{:T(128)} %constant.74.clone.1), kind=kCustom, calls=%fused_computation.50 | custom fusion | bytes 6148 | tf_op jit(solution)/shard_map/scatter | solution.py:27
  12.9 0.7 all_to_all.9
  13.6 7.3 %all-to-all-start = ((s32[8,1,192]{2,1,0:T(1,128)}), s32[8,1,192]{2,1,0:T(1,128)S(1)}, u32[]{:S(2)}, u32[]{:S(2)}) async-start(s32[8,1,192]{2,1,0:T(1,128)} %all_to_all.9), calls=%async_computation | async-start | bytes 16384 | tf_op jit(solution)/shard_map/all_to_all | solution.py:31
  20.8 0.7 compare_select_fusion.1
  21.5 0.8 reshape.166
  22.3 0.7 maximum_bitcast_fusion
  23.0 0.2 copy.26
  23.2 4.4 %scatter_custom_fusion.1 = f32[6,1536]{0,1:T(8,128)S(1)} fusion(s32[768]{0:T(1024)S(1)} %compare_select_fusion.2, f32[768,6]{1,0:T(8,128)S(1)} %copy.26, f32[]{:T(128)} %constant.39.clone.1), kind=kCustom, calls=%fused_computation.7 | custom fusion | bytes 36868 | tf_op jit(solution)/shard_map/scatter | solution.py:25
  27.6 1.0 copy.27
  28.6 0.9 convert_element_type.18
  29.5 14.5 %all_gather.3 = bf16[1024,128]{1,0:T(8,128)(2,1)S(1)} all-gather(bf16[256,128]{1,0:T(8,128)(2,1)S(1)} %convert_element_type.18), channel_id=1, replica_groups=mesh['parts'=2,'track'=4,'tm'=2,'coef'=2] {'track'}, dimensions={0}, use_global_device_ids=true | all-gather | bytes 327680 | tf_op jit(solution)/shard_map/all_gather | solution.py:18
  44.0 0.1 reshape.175
  44.0 0.6 gather_fusion
  44.7 0.8 compare_and_fusion
  45.4 0.1 select_bitcast_fusion
  45.5 3.7 %fusion = f32[8,1,3,128,1]{3,1,4,2,0:T(1,128)S(1)} fusion(bf16[8,6,3,128,128]{4,3,2,1,0:T(8,128)(2,1)} %param.13, bf16[8,6,128,1,1]{2,1,0,3,4:T(8,128)(2,1)S(1)} %select_bitcast_fusion), kind=kOutput, calls=%fused_computation.5 | convolution fusion | flops 4718592 | bytes 4743168 | tf_op jit(solution)/shard_map/skcjb,skb->scj/dot_general | solution.py:50
  49.2 3.3 %psum.14 = f32[8,3,128]{2,0,1:T(8,128)S(1)} all-reduce(f32[8,3,128]{2,0,1:T(8,128)S(1)} %bitcast.50), channel_id=1, replica_groups=mesh['parts'=2,'track'=4,'tm'=2,'coef'=2] {'coef'}, use_global_device_ids=true, to_apply=%region_9.10 | all-reduce | flops 3072 | bytes 24576 | tf_op jit(solution)/shard_map/psum | solution.py:53
  52.5 5.7 %all-to-all-start.1 = ((f32[8,6,192]{2,1,0:T(8,128)}), f32[8,6,192]{2,1,0:T(8,128)S(1)}, u32[]{:S(2)}, u32[]{:S(2)}) async-start(f32[8,6,192]{2,1,0:T(8,128)} %bitcast.8), calls=%async_computation.1 | async-start | bytes 131072 | tf_op jit(solution)/shard_map/all_to_all | solution.py:30
  58.2 0.0 reduce-scatter.2.cloned.1.call-start
  58.3 0.1 eq.61
  58.4 0.1 eq.57
  58.5 2.3 %reduce-window.16 = s32[8,12,128]{2,1,0:T(8,128)S(1)} reduce-window(s32[8,12,128]{2,1,0:T(8,128)S(1)} %fusion.8, s32[]{:T(128)} %constant.40.clone.1), window={size=1x1x128 pad=0_0x0_0x127_0}, to_apply=%region_4.5 | reduce-window | flops 1560576 | bytes 98308 | tf_op jit(solution)/shard_map/reduce-window.2
  60.7 0.3 slice_reduce_fusion
  61.0 0.2 reduce-window.19
  61.2 0.1 add_bitcast_fusion
  61.3 0.1 mul.43
  61.4 0.1 ge.21
  61.6 3.5 %all-to-all-done.1 = f32[8,6,192]{2,1,0:T(8,128)S(1)} async-done(((f32[8,6,192]{2,1,0:T(8,128)}), f32[8,6,192]{2,1,0:T(8,128)S(1)}, u32[]{:S(2)}, u32[]{:S(2)}) %all-to-all-start.1) | async-done | bytes 36896 | tf_op jit(solution)/shard_map/all_to_all | solution.py:30
  65.1 0.1 reshape.198
  65.2 0.3 copy.29
  65.5 4.4 %scatter_custom_fusion.2 = f32[6,1025]{0,1:T(8,128)S(1)} fusion(s32[1536]{0:T(1024)S(1)} %fusion.17, f32[1536,6]{1,0:T(8,128)S(1)} %copy.29, f32[]{:T(128)} %constant.39.clone.1), kind=kCustom, calls=%fused_computation.9 | custom fusion | bytes 24604 | tf_op jit(solution)/shard_map/scatter | solution.py:42
  70.0 0.2 copy.36
  70.2 3.1 %fusion.15 = f32[8,1,6,128,1]{3,1,4,2,0:T(1,128)S(1)} fusion(bf16[8,6,3,128,128]{4,3,2,1,0:T(8,128)(2,1)} %param.13, bf16[8,3,128,1,1]{2,0,1,3,4:T(8,128)(2,1)S(1)} %fusion.18), kind=kOutput, calls=%fused_computation.34 | convolution fusion | flops 4718592 | bytes 4749312 | tf_op jit(solution)/shard_map/skcjb,scj->skb/dot_general | solution.py:56
  73.3 0.1 bitcast_select_fusion
  73.4 1.5 %scatter_custom_fusion.3 = f32[1024,128]{1,0:T(8,128)} fusion(s32[48]{0:T(128)S(1)} %fusion.23, f32[48,128]{1,0:T(8,128)S(1)} %reshape.209, f32[]{:T(128)} %constant.39.clone.1), kind=kCustom, calls=%fused_computation.11 | custom fusion | flops 6144 | bytes 524292 | tf_op jit(solution)/shard_map/scatter-add | solution.py:60
  74.9 0.0 reduce-scatter.2.cloned.1.call-update
  75.0 0.0 all-reduce.2.cloned.1.call-start
  75.0 19.6 %reduce-scatter.2.cloned.1.call-done = f32[256,128]{1,0:T(8,128)} async-done(((f32[1024,128]{1,0:T(8,128)}), f32[256,128]{1,0:T(8,128)}) %reduce-scatter.2.cloned.1.call-update) | async-done | bytes 131088 | tf_op jit(solution)/shard_map/reduce_scatter | solution.py:61
  94.6 0.0 all-reduce.2.cloned.1.call-update
  94.7 32.0 %all-reduce.2.cloned.1.call-done = f32[256,128]{1,0:T(8,128)} async-done(((f32[256,128]{1,0:T(8,128)}), f32[256,128]{1,0:T(8,128)}) %all-reduce.2.cloned.1.call-update) | async-done | bytes 131088 | tf_op jit(solution)/shard_map/psum | solution.py:62
  126.6 1.6 %copy.49 = f32[256,128]{1,0:T(8,128)} copy(f32[256,128]{1,0:T(8,128)} %all-reduce.2.cloned.1.call-done) | data formatting | bytes 262144
  (17 shorter events, 0.3 us)
Async XLA Ops:
  13.6 38.9 %all-to-all-start = ((s32[8,1,192]{2,1,0:T(1,128)}), s32[8,1,192]{2,1,0:T(1,128)S(1)}, u32[]{:S(2)}, u32[]{:S(2)}) async-start(s32[8,1,192]{2,1,0:T(1,128)} %all_to_all.9), calls=%async_computation | async-start | bytes 16384 | tf_op jit(solution)/shard_map/all_to_all | solution.py:31
  52.5 12.6 %all-to-all-start.1 = ((f32[8,6,192]{2,1,0:T(8,128)}), f32[8,6,192]{2,1,0:T(8,128)S(1)}, u32[]{:S(2)}, u32[]{:S(2)}) async-start(f32[8,6,192]{2,1,0:T(8,128)} %bitcast.8), calls=%async_computation.1 | async-start | bytes 131072 | tf_op jit(solution)/shard_map/all_to_all | solution.py:30
  58.2 36.4 %reduce-scatter.2.cloned.1.call-start = ((), (), s32[]{:S(2)}) async-start(), calls=%async_computation.3 | async-start | bytes 655360 | tf_op jit(solution)/shard_map/reduce_scatter | solution.py:61
  75.0 51.7 %all-reduce.2.cloned.1.call-start = ((), (), s32[]{:S(2)}) async-start(), calls=%async_computation.4 | async-start | bytes 262144 | tf_op jit(solution)/shard_map/psum | solution.py:62
Sparse Core Ops, SparseCore 0:
  75.1 19.5 reduce-scatter.1
  97.0 29.6 all-reduce.1
where the time goes:
time: 136 us; the launch traced here: 135 us
  waiting for transfers between devices  55.2 us (41%)
  local copies, waits for them, and re-layouts  18.6 us (14%)
  blocking collectives  17.8 us (13%)
  between operations  13.5 us (10%)
  starting transfers between devices  13.1 us (10%)
  other arithmetic  10.2 us (7%)
  matrix products  6.73 us (5%)
    psum x1, waiting for transfers between devices, per_device(): gradient = lax.psum(summed, ('tm', 'coef'))  32 us
    reduce_scatter x1, waiting for transfers between devices, per_device(): lax.psum_scatter(partial_grad, 'track', scatter_dimension=0, tiled=True)  19.6 us
    all_gather x1, blocking collectives, per_device(): every_block = lax.all_gather(rounded, 'track', axis=0, tiled=True)  14.5 us
    all_to_all x1, starting transfers between devices, per_device(): lax.all_to_all(labels, ('track', 'tm'), split_axis=0, concat_axis=0, tile...  7.25 us
    all_to_all x1, starting transfers between devices, per_device(): lax.all_to_all(outgoing, ('track', 'tm'), split_axis=0, concat_axis=0, ti...  5.72 us
    scatter x1, local copies, waits for them, and re-layouts, per_device(): jnp.zeros((6, sector_total * slot_count + 1), jnp.float32).at[:, target]  4.45 us
    scatter x1, local copies, waits for them, and re-layouts, per_device(): jnp.zeros((6, owners * capacity), jnp.float32).at[:, placing].set(payload)  4.36 us
    another operation x4, other arithmetic  4.31 us
  transfers between devices with their start and end apart: 4, of which 3 were waited for; matrix products, arithmetic and copies ran while one was open for 13% of the time, Pallas kernels for 0%

commit v1 on v0

--- a/solution.py
+++ b/solution.py
@@ -4,6 +4,12 @@
 from jax.sharding import PartitionSpec as P
 
 HUBER = 2.0
+
+
+def joined_along(tiles, dim):
+    shape = list(tiles.shape[1:])
+    shape[dim] *= tiles.shape[0]
+    return jnp.moveaxis(tiles, 0, dim).reshape(shape)
 
 
 def per_device(sector_ids, observed, weights, coefficients, tile_index, tile_count, sensitivity):
@@ -15,7 +21,19 @@
     row_total = sector_ids.shape[0]
     capacity = 2 * row_total // owners
     rounded = coefficients.astype(jnp.bfloat16)
-    every_block = lax.all_gather(rounded, "track", axis=0, tiled=True)
+    length = lax.axis_size("track")
+    pairs = [(i, (i + 1) % length) for i in range(length)]
+    back = [(b, a) for a, b in pairs]
+    lower, upper = ([], [])
+    for step in range(length - 1):
+        if step % 2 == 0:
+            lower.append(lax.ppermute(lower[-1] if lower else rounded, "track", pairs))
+        else:
+            upper.append(lax.ppermute(upper[-1] if upper else rounded, "track", back))
+    parts = jnp.stack([*lower[::-1], rounded, *upper])
+    shift = lax.axis_index("track") - len(lower)
+    parts = parts[(jnp.arange(length) - shift) % length]
+    every_block = joined_along(parts, 0)
     owner_of = sector_ids // sector_total
     local_sector = sector_ids % sector_total
     onehot = (owner_of[:, None] == jnp.arange(owners, dtype=jnp.int32)[None, :]).astype(jnp.int32)

time: 136 us -> 126 us (0.926)
  blocking collectives: 17.8 us -> 3.3 us
  starting transfers between devices: 13.1 us -> 17.4 us
  waiting for transfers between devices: 55.2 us -> 53.8 us
    all_gather x1 -> x0, blocking collectives: 14.5 us -> none  [per_device(): every_block = lax.all_gather(rounded, 'track', axis=0, tiled=True)]
    ppermute x0 -> x3, starting transfers between devices: none -> 7.14 us  [the longest x2 5.05 us: per_device(): lower.append(lax.ppermute(lower[-1] if lower else rounded, 'track', pairs))]
    all_to_all x1, starting transfers between devices: 7.25 us -> 4.17 us  [per_device(): lax.all_to_all(labels, ('track', 'tm'), split_axis=0, concat_axis=0, tile...]
    all_to_all x1, waiting for transfers between devices: 3.54 us -> 1.51 us  [per_device(): lax.all_to_all(outgoing, ('track', 'tm'), split_axis=0, concat_axis=0, ti...]
    another operation x4 -> x6, other arithmetic: 4.31 us -> 5.26 us
  transfers between devices with their start and end apart: 4 -> 7, of which waited for: 3 -> 3; matrix products, arithmetic and copies ran while one was open for 13% -> 19% of each run, Pallas kernels for 0% -> 0%
where the time goes in v1:
time: 126 us; the launch traced here: 125 us
  waiting for transfers between devices  53.8 us (43%)
  local copies, waits for them, and re-layouts  19.2 us (15%)
  starting transfers between devices  17.4 us (14%)
  between operations  13.6 us (11%)
  other arithmetic  11.1 us (9%)
  matrix products  6.73 us (5%)
  blocking collectives  3.3 us (3%)
    psum x1, waiting for transfers between devices, per_device(): gradient = lax.psum(summed, ('tm', 'coef'))  31.9 us
    reduce_scatter x1, waiting for transfers between devices, per_device(): lax.psum_scatter(partial_grad, 'track', scatter_dimension=0, tiled=True)  20.3 us
    all_to_all x1, starting transfers between devices, per_device(): lax.all_to_all(outgoing, ('track', 'tm'), split_axis=0, concat_axis=0, ti...  6 us
    ppermute x2, starting transfers between devices, per_device(): lower.append(lax.ppermute(lower[-1] if lower else rounded, 'track', pairs))  5.05 us
    scatter x1, local copies, waits for them, and re-layouts, per_device(): jnp.zeros((6, sector_total * slot_count + 1), jnp.float32).at[:, target]  4.45 us
    scatter x1, local copies, waits for them, and re-layouts, per_device(): jnp.zeros((6, owners * capacity), jnp.float32).at[:, placing].set(payload)  4.36 us
    another operation x4, other arithmetic  4.31 us
    all_to_all x1, starting transfers between devices, per_device(): lax.all_to_all(labels, ('track', 'tm'), split_axis=0, concat_axis=0, tile...  4.17 us
  transfers between devices with their start and end apart: 7, of which 3 were waited for; matrix products, arithmetic and copies ran while one was open for 19% of the time, Pallas kernels for 0%

profile of v1, /device:TPU:0, one launch (start us, length us, event | category | flops | bytes accessed | tf_op | source)
XLA Modules:
  0.0 125.1 jit_solution(17426266086211105092)
XLA Ops:
  6.5 0.9 convert_element_type.18
  7.4 3.0 %collective-permute-start = (bf16[256,128]{1,0:T(8,128)(2,1)S(1)}, bf16[256,128]{1,0:T(8,128)(2,1)S(1)}, u32[]{:S(2)}, u32[]{:S(2)}) collective-permute-start(bf16[256,128]{1,0:T(8,128)(2,1)S(1)} %convert_element_type.18), channel_id=1, source_target_pairs={{0,4},{4,8},{8,12},{12,0},{1,5},{5,9},{9,13},{13,1},{2,6},{6,10},{... | collective-permute-start | bytes 196616 | tf_op jit(solution)/shard_map/ppermute | solution.py:30
  10.5 2.1 %collective-permute-start.2 = (bf16[256,128]{1,0:T(8,128)(2,1)S(1)}, bf16[256,128]{1,0:T(8,128)(2,1)S(1)}, u32[]{:S(2)}, u32[]{:S(2)}) collective-permute-start(bf16[256,128]{1,0:T(8,128)(2,1)S(1)} %convert_element_type.18), channel_id=1, source_target_pairs={{4,0},{8,4},{12,8},{0,12},{5,1},{9,5},{13,9},{1,13},{6,2},{10,6},{... | collective-permute-start | bytes 196616 | tf_op jit(solution)/shard_map/ppermute | solution.py:32
  12.6 0.7 add_select_fusion
  13.3 1.7 %reduce-window.14 = s32[8,6,128]{2,0,1:T(8,128)S(1)} reduce-window(s32[8,6,128]{2,0,1:T(8,128)S(1)} %fusion.13, s32[]{:T(128)} %constant.54.clone.1), window={size=1x1x128 pad=0_0x0_0x127_0}, to_apply=%region_0.1 | reduce-window | flops 780288 | bytes 49156 | tf_op jit(solution)/shard_map/reduce-window
  15.0 0.1 slice.32
  15.0 0.1 copy.24
  15.2 0.2 reduce-window.15
  15.3 0.1 copy.25
  15.4 0.1 fusion.11
  15.5 3.4 %scatter_custom_fusion = s32[1536]{0:T(1024)S(1)} fusion(s32[768]{0:T(1024)S(1)} %compare_select_fusion.2, s32[768]{0:T(1024)S(1)} %get-tuple-element.7, s32[]{:T(128)} %constant.93.clone.1), kind=kCustom, calls=%fused_computation.53 | custom fusion | bytes 6148 | tf_op jit(solution)/shard_map/scatter | solution.py:45
  18.9 0.7 all_to_all.9
  19.6 4.2 %all-to-all-start = ((s32[8,1,192]{2,1,0:T(1,128)}), s32[8,1,192]{2,1,0:T(1,128)S(1)}, u32[]{:S(2)}, u32[]{:S(2)}) async-start(s32[8,1,192]{2,1,0:T(1,128)} %all_to_all.9), calls=%async_computation | async-start | bytes 16384 | tf_op jit(solution)/shard_map/all_to_all | solution.py:49
  23.8 0.9 convert_bitcast_fusion
  24.7 0.7 compare_select_fusion.1
  25.4 0.8 reshape.218
  26.2 0.1 reshape.236
  26.3 0.7 maximum_bitcast_fusion
  27.0 0.8 compare_and_fusion
  27.8 0.2 copy.26
  28.0 4.4 %scatter_custom_fusion.1 = f32[6,1536]{0,1:T(8,128)S(1)} fusion(s32[768]{0:T(1024)S(1)} %compare_select_fusion.2, f32[768,6]{1,0:T(8,128)S(1)} %copy.26, f32[]{:T(128)} %constant.53.clone.1), kind=kCustom, calls=%fused_computation.8 | custom fusion | bytes 36868 | tf_op jit(solution)/shard_map/scatter | solution.py:43
  32.3 1.0 copy.27
  33.3 6.0 %all-to-all-start.1 = ((f32[8,6,192]{2,1,0:T(8,128)}), f32[8,6,192]{2,1,0:T(8,128)S(1)}, u32[]{:S(2)}, u32[]{:S(2)}) async-start(f32[8,6,192]{2,1,0:T(8,128)} %bitcast.8), calls=%async_computation.1 | async-start | bytes 131072 | tf_op jit(solution)/shard_map/all_to_all | solution.py:48
  39.4 0.1 eq.63
  39.5 0.1 eq.59
  39.5 2.3 %reduce-window.16 = s32[8,12,128]{2,1,0:T(8,128)S(1)} reduce-window(s32[8,12,128]{2,1,0:T(8,128)S(1)} %fusion.8, s32[]{:T(128)} %constant.54.clone.1), window={size=1x1x128 pad=0_0x0_0x127_0}, to_apply=%region_4.5 | reduce-window | flops 1560576 | bytes 98308 | tf_op jit(solution)/shard_map/reduce-window.2
  41.8 0.3 slice_reduce_fusion
  42.1 0.2 reduce-window.19
  42.3 0.1 add_bitcast_fusion
  42.4 0.1 mul.43
  42.5 0.1 ge.21
  42.6 2.0 %collective-permute-start.1 = (bf16[256,128]{1,0:T(8,128)(2,1)S(1)}, bf16[256,128]{1,0:T(8,128)(2,1)S(1)}, u32[]{:S(2)}, u32[]{:S(2)}) collective-permute-start(bf16[256,128]{1,0:T(8,128)(2,1)S(1)} %collective-permute-done), channel_id=1, source_target_pairs={{0,4},{4,8},{8,12},{12,0},{1,5},{5,9},{9,13},{13,1},{2,6},{6,10},{... | collective-permute-start | bytes 196616 | tf_op jit(solution)/shard_map/ppermute | solution.py:30
  44.7 1.5 %all-to-all-done.1 = f32[8,6,192]{2,1,0:T(8,128)S(1)} async-done(((f32[8,6,192]{2,1,0:T(8,128)}), f32[8,6,192]{2,1,0:T(8,128)S(1)}, u32[]{:S(2)}, u32[]{:S(2)}) %all-to-all-start.1) | async-done | bytes 36896 | tf_op jit(solution)/shard_map/all_to_all | solution.py:48
  46.2 0.1 reshape.259
  46.3 0.3 copy.29
  46.6 4.4 %scatter_custom_fusion.2 = f32[6,1025]{0,1:T(8,128)S(1)} fusion(s32[1536]{0:T(1024)S(1)} %fusion.17, f32[1536,6]{1,0:T(8,128)S(1)} %copy.29, f32[]{:T(128)} %constant.53.clone.1), kind=kCustom, calls=%fused_computation.10 | custom fusion | bytes 24604 | tf_op jit(solution)/shard_map/scatter | solution.py:60
  51.1 0.2 copy.36
  51.4 0.6 gather_fusion
  52.0 0.6 gather_fusion.1
  52.6 0.1 select_bitcast_fusion
  52.7 3.7 %fusion = f32[8,1,3,128,1]{3,1,4,2,0:T(1,128)S(1)} fusion(bf16[8,6,3,128,128]{4,3,2,1,0:T(8,128)(2,1)} %param.13, bf16[8,6,128,1,1]{2,1,0,3,4:T(8,128)(2,1)S(1)} %select_bitcast_fusion), kind=kOutput, calls=%fused_computation.6 | convolution fusion | flops 4718592 | bytes 4743168 | tf_op jit(solution)/shard_map/skcjb,skb->scj/dot_general | solution.py:68
  56.3 3.3 %psum.14 = f32[8,3,128]{2,0,1:T(8,128)S(1)} all-reduce(f32[8,3,128]{2,0,1:T(8,128)S(1)} %bitcast.62), channel_id=1, replica_groups=mesh['parts'=2,'track'=4,'tm'=2,'coef'=2] {'coef'}, use_global_device_ids=true, to_apply=%region_9.10 | all-reduce | flops 3072 | bytes 24576 | tf_op jit(solution)/shard_map/psum | solution.py:71
  59.7 3.1 %fusion.15 = f32[8,1,6,128,1]{3,1,4,2,0:T(1,128)S(1)} fusion(bf16[8,6,3,128,128]{4,3,2,1,0:T(8,128)(2,1)} %param.13, bf16[8,3,128,1,1]{2,0,1,3,4:T(8,128)(2,1)S(1)} %fusion.18), kind=kOutput, calls=%fused_computation.36 | convolution fusion | flops 4718592 | bytes 4749312 | tf_op jit(solution)/shard_map/skcjb,scj->skb/dot_general | solution.py:74
  62.7 0.1 bitcast_select_fusion
  62.8 1.5 %scatter_custom_fusion.3 = f32[1024,128]{1,0:T(8,128)} fusion(s32[48]{0:T(128)S(1)} %fusion.24, f32[48,128]{1,0:T(8,128)S(1)} %reshape.270, f32[]{:T(128)} %constant.53.clone.1), kind=kCustom, calls=%fused_computation.13 | custom fusion | flops 6144 | bytes 524292 | tf_op jit(solution)/shard_map/scatter-add | solution.py:78
  64.4 20.3 %reduce-scatter.2.cloned.1.call-done = f32[256,128]{1,0:T(8,128)} async-done(((f32[1024,128]{1,0:T(8,128)}), f32[256,128]{1,0:T(8,128)}) %reduce-scatter.2.cloned.1.call-update) | async-done | bytes 131088 | tf_op jit(solution)/shard_map/reduce_scatter | solution.py:79
  84.7 31.9 %all-reduce.2.cloned.1.call-done = f32[256,128]{1,0:T(8,128)} async-done(((f32[256,128]{1,0:T(8,128)}), f32[256,128]{1,0:T(8,128)}) %all-reduce.2.cloned.1.call-update) | async-done | bytes 131088 | tf_op jit(solution)/shard_map/psum | solution.py:80
  116.7 1.6 %copy.49 = f32[256,128]{1,0:T(8,128)} copy(f32[256,128]{1,0:T(8,128)} %all-reduce.2.cloned.1.call-done) | data formatting | bytes 262144
  (27 shorter events, 0.5 us)
Async XLA Ops:
  7.4 35.2 %collective-permute-start = (bf16[256,128]{1,0:T(8,128)(2,1)S(1)}, bf16[256,128]{1,0:T(8,128)(2,1)S(1)}, u32[]{:S(2)}, u32[]{:S(2)}) collective-permute-start(bf16[256,128]{1,0:T(8,128)(2,1)S(1)} %convert_element_type.18), channel_id=1, source_target_pairs={{0,4},{4,8},{8,12},{12,0},{1,5},{5,9},{9,13},{13,1},{2,6},{6,10},{... | collective-permute-start | bytes 196616 | tf_op jit(solution)/shard_map/ppermute | solution.py:30
  10.5 40.8 %collective-permute-start.2 = (bf16[256,128]{1,0:T(8,128)(2,1)S(1)}, bf16[256,128]{1,0:T(8,128)(2,1)S(1)}, u32[]{:S(2)}, u32[]{:S(2)}) collective-permute-start(bf16[256,128]{1,0:T(8,128)(2,1)S(1)} %convert_element_type.18), channel_id=1, source_target_pairs={{4,0},{8,4},{12,8},{0,12},{5,1},{9,5},{13,9},{1,13},{6,2},{10,6},{... | collective-permute-start | bytes 196616 | tf_op jit(solution)/shard_map/ppermute | solution.py:32
  19.6 13.7 %all-to-all-start = ((s32[8,1,192]{2,1,0:T(1,128)}), s32[8,1,192]{2,1,0:T(1,128)S(1)}, u32[]{:S(2)}, u32[]{:S(2)}) async-start(s32[8,1,192]{2,1,0:T(1,128)} %all_to_all.9), calls=%async_computation | async-start | bytes 16384 | tf_op jit(solution)/shard_map/all_to_all | solution.py:49
  33.3 12.9 %all-to-all-start.1 = ((f32[8,6,192]{2,1,0:T(8,128)}), f32[8,6,192]{2,1,0:T(8,128)S(1)}, u32[]{:S(2)}, u32[]{:S(2)}) async-start(f32[8,6,192]{2,1,0:T(8,128)} %bitcast.8), calls=%async_computation.1 | async-start | bytes 131072 | tf_op jit(solution)/shard_map/all_to_all | solution.py:48
  39.3 45.4 %reduce-scatter.2.cloned.1.call-start = ((), (), s32[]{:S(2)}) async-start(), calls=%async_computation.3 | async-start | bytes 655360 | tf_op jit(solution)/shard_map/reduce_scatter | solution.py:79
  42.6 8.7 %collective-permute-start.1 = (bf16[256,128]{1,0:T(8,128)(2,1)S(1)}, bf16[256,128]{1,0:T(8,128)(2,1)S(1)}, u32[]{:S(2)}, u32[]{:S(2)}) collective-permute-start(bf16[256,128]{1,0:T(8,128)(2,1)S(1)} %collective-permute-done), channel_id=1, source_target_pairs={{0,4},{4,8},{8,12},{12,0},{1,5},{5,9},{9,13},{13,1},{2,6},{6,10},{... | collective-permute-start | bytes 196616 | tf_op jit(solution)/shard_map/ppermute | solution.py:30
  64.4 52.3 %all-reduce.2.cloned.1.call-start = ((), (), s32[]{:S(2)}) async-start(), calls=%async_computation.4 | async-start | bytes 262144 | tf_op jit(solution)/shard_map/psum | solution.py:80
Sparse Core Ops, SparseCore 0:
  64.5 20.1 reduce-scatter.1
  87.0 29.5 all-reduce.1
